TPU v7x, 32 devices: a whole 2x2x4 slice. The times are simulated.
32 devices in a mesh: group: 2 (over x), tensor: 16 (over z, y, core).
Axes of the slice: x: 2, y: 2, z: 4, core: 2. Of those that a mesh axis runs over, the one named last changes fastest.
Arguments:
- tokens_in: bfloat16 [64, 5120], P('group', 'tensor'), parts along dimension 0, may hold values from -20 to 20
- norm_gain: float32 [5120], P('tensor'), may hold values from 0.1 to 1.9
- w_qkv: bfloat16 [5120, 7168], P('tensor'), may hold values from -0.078125 to 0.078125
- w_out: bfloat16 [5120, 5120], P(None, 'tensor'), may hold values from -0.078125 to 0.078125
- cache_keys: bfloat16 [64, 96, 1024], P(('group', 'tensor')), parts along dimension 0, may hold values from -240 to 240
- cache_values: bfloat16 [64, 96, 1024], P(('group', 'tensor')), parts along dimension 0, may hold values from -6 to 6
- kv_lengths: int32 [64], P(('group', 'tensor')), parts along dimension 0, may hold values from 1 to 96
- w_cond: bfloat16 [5120, 1536], P('tensor'), may hold values from -0.078125 to 0.078125
- w_embed: bfloat16 [16, 5120], P(None, 'tensor'), may hold values from -1.5 to 1.5
- placement: int32 [64, 1], P('group'), parts along dimension 0, may hold values from 0 to 15; in each aligned block of 32 rows (0 to 31, 32 to 63, ...) at most 8 rows name the same one
- noise: float32 [2, 256, 16], P(None, ('group', 'tensor')), parts along dimension 1, may hold values from -5 to 5
- w_latent: bfloat16 [16, 1536], replicated, may hold values from -1.5 to 1.5
- w_up: bfloat16 [1536, 1536], replicated, may hold values from -0.15625 to 0.15625
- w_down: bfloat16 [1536, 1536], replicated, may hold values from -0.15625 to 0.15625
- w_vel: bfloat16 [1536, 16], replicated, may hold values from -0.15625 to 0.15625
- head_gain: float32 [1536], replicated, may hold values from 0.1 to 1.9
Outputs:
- latents: float32 [2, 64, 16], P(None, ('group', 'tensor')), parts along dimension 1
- hidden: bfloat16 [64, 5120], P('group', 'tensor'), parts along dimension 0
There are 2 independent parts, one for each index of `group`. A program takes and returns all parts, laid end to end along the dimension named above; an argument that names none is the same for every part. Nothing has to cross between parts.
Inputs may be any that keep to these rules, and one draw needn't show every extreme that they name: `placement`: at most 8 requests share a head device, and one head device has exactly 8.
All inputs are finite; a program needn't handle non-finite values.
Results may differ from a plain program's by a relative error of at most 0.025.
Values may be sent and summed in bfloat16 or wider, within the bound.
A program may use at most 64 MiB of HBM per device.

v0:
```python
import math

import jax
import jax.numpy as jnp
from jax import lax
from jax.sharding import PartitionSpec as P

D = 5120
HEADS = 40
KVH = 8
HD = 128
HW = 1536
STEPS = 8
HCAP = 8


def slot_numbers(placement, devices):
    owner = placement[:, 0]
    onehot = (owner[:, None] == jnp.arange(devices, dtype=jnp.int32)[None, :]).astype(jnp.int32)
    before = jnp.cumsum(onehot, axis=0) - onehot
    rank = jnp.sum(before * onehot, axis=1)
    return owner * HCAP + rank


def time_table(number):
    half = HW // 2
    freqs = jnp.exp(-math.log(10000.0) * jnp.arange(half, dtype=jnp.float32) / half)
    angle = 1000.0 * number / STEPS * freqs
    return jnp.concatenate([jnp.sin(angle), jnp.cos(angle)])


def denoise(latent, condition, w_latent, w_up, w_down, w_vel, head_gain):
    for number in range(STEPS):
        act = jnp.dot(latent.astype(jnp.bfloat16), w_latent, preferred_element_type=jnp.float32)
        act = act + condition.astype(jnp.float32) + time_table(number)[None, :]
        normact = (
            act * lax.rsqrt(jnp.mean(act * act, axis=1, keepdims=True) + 1e-05) * head_gain
        ).astype(jnp.bfloat16)
        inner = jax.nn.silu(jnp.dot(normact, w_up, preferred_element_type=jnp.float32)).astype(
            jnp.bfloat16
        )
        block = act + jnp.dot(inner, w_down, preferred_element_type=jnp.float32)
        normblock = (
            block * lax.rsqrt(jnp.mean(block * block, axis=1, keepdims=True) + 1e-05)
        ).astype(jnp.bfloat16)
        latent = latent + jnp.dot(normblock, w_vel, preferred_element_type=jnp.float32) / STEPS
    return latent


def attend(query, cache_keys, cache_values, lengths, extra_keys, extra_values):
    rows = query.shape[0]
    cached = cache_keys.shape[1]
    extra = extra_keys.shape[1]
    group = HEADS // KVH
    queries = query.reshape(rows, KVH, group, HD)
    keys_c = cache_keys.reshape(rows, cached, KVH, HD)
    vals_c = cache_values.reshape(rows, cached, KVH, HD)
    keys_e = extra_keys.reshape(rows, extra, KVH, HD)
    vals_e = extra_values.reshape(rows, extra, KVH, HD)
    scale = 1.0 / math.sqrt(HD)
    score_c = (
        jnp.einsum("rkgd,rckd->rkgc", queries, keys_c, preferred_element_type=jnp.float32) * scale
    )
    live = jnp.arange(cached, dtype=jnp.int32)[None, :] < lengths[:, None]
    score_c = jnp.where(live[:, None, None, :], score_c, -1e30)
    score_e = (
        jnp.einsum("rkgd,rekd->rkge", queries, keys_e, preferred_element_type=jnp.float32) * scale
    )
    top = jnp.maximum(jnp.max(score_c, axis=3), jnp.max(score_e, axis=3))
    prob_c = jnp.exp(score_c - top[..., None])
    prob_e = jnp.exp(score_e - top[..., None])
    total = jnp.sum(prob_c, axis=3) + jnp.sum(prob_e, axis=3)
    weight_c = (prob_c / total[..., None]).astype(jnp.bfloat16)
    weight_e = (prob_e / total[..., None]).astype(jnp.bfloat16)
    mixed = jnp.einsum("rkgc,rckd->rkgd", weight_c, vals_c, preferred_element_type=jnp.float32)
    mixed = mixed + jnp.einsum(
        "rkge,rekd->rkgd", weight_e, vals_e, preferred_element_type=jnp.float32
    )
    return mixed.reshape(rows, HEADS * HD).astype(jnp.bfloat16)


def per_device(
    tokens_in,
    norm_gain,
    w_qkv,
    w_out,
    cache_keys,
    cache_values,
    kv_lengths,
    w_cond,
    w_embed,
    placement,
    noise,
    w_latent,
    w_up,
    w_down,
    w_vel,
    head_gain,
):
    devices = lax.axis_size("tensor")
    position = lax.axis_index("tensor")
    own_rows = cache_keys.shape[0]
    slot = slot_numbers(placement, devices)
    inputs = tokens_in
    extra_keys = jnp.zeros((own_rows, 0, KVH * HD), jnp.bfloat16)
    extra_values = jnp.zeros((own_rows, 0, KVH * HD), jnp.bfloat16)
    results = []
    decoded = inputs
    for decode_index in range(2):
        floats = inputs.astype(jnp.float32)
        squares = lax.psum(jnp.sum(floats * floats, axis=1), "tensor")
        rms = jnp.sqrt(squares / D + 1e-06)
        normed = (floats * norm_gain[None, :] / rms[:, None]).astype(jnp.bfloat16)
        qkv = lax.psum_scatter(
            jnp.dot(normed, w_qkv, preferred_element_type=jnp.float32),
            "tensor",
            scatter_dimension=0,
            tiled=True,
        ).astype(jnp.bfloat16)
        query = qkv[:, : HEADS * HD]
        new_key = qkv[:, HEADS * HD : (HEADS + KVH) * HD]
        new_value = qkv[:, (HEADS + KVH) * HD :]
        extra_keys = jnp.concatenate([extra_keys, new_key[:, None, :]], axis=1)
        extra_values = jnp.concatenate([extra_values, new_value[:, None, :]], axis=1)
        attended = attend(query, cache_keys, cache_values, kv_lengths, extra_keys, extra_values)
        projected = jnp.dot(
            lax.all_gather(attended, "tensor", axis=0, tiled=True),
            w_out,
            preferred_element_type=jnp.float32,
        )
        decoded = (floats + projected).astype(jnp.bfloat16)
        cond_all = lax.psum(
            jnp.dot(decoded, w_cond, preferred_element_type=jnp.float32), "tensor"
        ).astype(jnp.bfloat16)
        wanted = position * HCAP + jnp.arange(HCAP, dtype=jnp.int32)
        picker = (slot[None, :] == wanted[:, None]).astype(jnp.bfloat16)
        condition = jnp.dot(picker, cond_all, preferred_element_type=jnp.float32).astype(
            jnp.bfloat16
        )
        latent = denoise(noise[decode_index], condition, w_latent, w_up, w_down, w_vel, head_gain)
        slots_all = lax.all_gather(latent, "tensor", axis=0, tiled=True)
        latent_all = slots_all[slot]
        own_latent = lax.dynamic_slice_in_dim(latent_all, position * own_rows, own_rows)
        results.append(own_latent)
        inputs = jnp.dot(
            latent_all.astype(jnp.bfloat16), w_embed, preferred_element_type=jnp.float32
        ).astype(jnp.bfloat16)
    return (jnp.stack(results), decoded)


def solution(mesh):
    return jax.shard_map(
        per_device,
        mesh=mesh,
        in_specs=(
            P("group", "tensor"),
            P("tensor"),
            P("tensor", None),
            P(None, "tensor"),
            P(("group", "tensor"), None, None),
            P(("group", "tensor"), None, None),
            P(("group", "tensor")),
            P("tensor", None),
            P(None, "tensor"),
            P("group", None),
            P(None, ("group", "tensor"), None),
            P(),
            P(),
            P(),
            P(),
            P(),
        ),
        out_specs=(P(None, ("group", "tensor"), None), P("group", "tensor")),
        check_vma=False,
    )
```

profile of v0, /device:TPU:0, one launch (start us, length us, event | category | flops | bytes accessed | tf_op | source)
XLA Modules:
  0.0 559.3 jit_solution(1993590594675003805)
XLA Ops:
  1.2 1.5 dynamic-slice
  3.3 0.7 iota_compare_fusion.1
  4.1 0.9 fusion.58
  4.9 34.9 %psum.28 = f32[32]{0:T(128)S(1)} all-reduce(f32[32]{0:T(128)S(1)} %fusion.58), channel_id=1, replica_groups=mesh['group'=2,'tensor'=16] {'tensor'}, use_global_device_ids=true, to_apply=%region_3.4 | all-reduce | flops 32 | bytes 256 | tf_op jit(solution)/shard_map/psum | solution.py:111
  43.4 0.7 fusion.182
  44.2 0.8 select_reduce_fusion
  45.0 1.2 multiply_add_fusion
  47.4 4.2 fusion.63
  51.6 68.8 %all-reduce.6 = bf16[32,7168]{1,0:T(8,128)(2,1)} all-reduce(f32[32,7168]{1,0:T(8,128)} %fusion.63), channel_id=2, replica_groups=mesh['group'=2,'tensor'=16] {'tensor'}, use_global_device_ids=true, to_apply=%region_4.5.clone | all-reduce | flops 229376 | bytes 1376256
  120.4 0.9 dynamic-slice_convert_fusion.1
  122.8 1.4 fusion.260
  124.4 1.3 fusion.21
  125.7 19.4 %all-gather = bf16[16,2,5120]{2,1,0:T(2,128)(2,1)} all-gather(bf16[1,2,5120]{2,1,0:T(2,128)(2,1)S(1)} %reshape.391), channel_id=1, replica_groups=mesh['group'=2,'tensor'=16] {'tensor'}, dimensions={0}, use_global_device_ids=true | all-gather | bytes 348160 | tf_op jit(solution)/shard_map/all_gather | solution.py:127
  145.1 1.8 reshape.392
  146.9 3.5 fusion.25
  150.4 61.7 %all-reduce.7 = bf16[32,1536]{1,0:T(8,128)(2,1)S(1)} all-reduce(f32[32,1536]{1,0:T(8,128)} %fusion.25), channel_id=1, replica_groups=mesh['group'=2,'tensor'=16] {'tensor'}, use_global_device_ids=true, to_apply=%region_7.8 | all-reduce | flops 49152 | bytes 294912 | tf_op jit(solution)/shard_map/psum | solution.py:132
  212.1 0.8 fusion.17
  212.9 1.0 multiply_reduce_fusion.32
  214.4 5.9 %multiply_reduce_fusion.31 = (f32[8]{0:T(128)}, f32[8,1536]{1,0:T(8,128)S(1)}) fusion(f32[8,1536]{1,0:T(8,128)S(1)} %get-tuple-element.12, bf16[1536,1536]{1,0:T(8,128)(2,1)} %param.29, bf16[1536,1536]{1,0:T(8,128)(2,1)} %param.28, f32[1536]{0:T(1024)S(1)} %copy-done.3, f32[8]{0:T(128)} %add_rsqrt_fusion.31), kind=kOutput, calls=%fused_computation.205 | convolution fusion | flops 75632632 | bytes 9541696 | tf_op jit(solution)/shard_map/dot_general | solution.py:42
  220.3 0.7 add_rsqrt_fusion.30
  220.9 0.9 fusion.41
  221.8 0.9 multiply_reduce_fusion.30
  223.3 5.8 %multiply_reduce_fusion.29 = (f32[8]{0:T(128)}, f32[8,1536]{1,0:T(8,128)S(1)}) fusion(f32[8,1536]{1,0:T(8,128)S(1)} %get-tuple-element.16, bf16[1536,1536]{1,0:T(8,128)(2,1)} %param.29, bf16[1536,1536]{1,0:T(8,128)(2,1)} %param.28, f32[8]{0:T(128)} %add_rsqrt_fusion.29, f32[1536]{0:T(1024)S(1)} %copy-done.3), kind=kOutput, calls=%fused_computation.200 | convolution fusion | flops 75632632 | bytes 9541696 | tf_op jit(solution)/shard_map/dot_general | solution.py:42
  229.7 0.9 fusion.40
  230.6 0.9 multiply_reduce_fusion.28
  232.0 5.8 %multiply_reduce_fusion.27 = (f32[8]{0:T(128)}, f32[8,1536]{1,0:T(8,128)S(1)}) fusion(f32[8,1536]{1,0:T(8,128)S(1)} %get-tuple-element.20, bf16[1536,1536]{1,0:T(8,128)(2,1)} %param.29, bf16[1536,1536]{1,0:T(8,128)(2,1)} %param.28, f32[8]{0:T(128)} %add_rsqrt_fusion.27, f32[1536]{0:T(1024)S(1)} %copy-done.3), kind=kOutput, calls=%fused_computation.195 | convolution fusion | flops 75632632 | bytes 9541696 | tf_op jit(solution)/shard_map/dot_general | solution.py:42
  238.4 0.9 fusion.39
  239.3 0.9 multiply_reduce_fusion.26
  240.8 5.8 %multiply_reduce_fusion.25 = (f32[8]{0:T(128)}, f32[8,1536]{1,0:T(8,128)S(1)}) fusion(f32[8,1536]{1,0:T(8,128)S(1)} %get-tuple-element.24, bf16[1536,1536]{1,0:T(8,128)(2,1)} %param.29, bf16[1536,1536]{1,0:T(8,128)(2,1)} %param.28, f32[8]{0:T(128)} %add_rsqrt_fusion.25, f32[1536]{0:T(1024)S(1)} %copy-done.3), kind=kOutput, calls=%fused_computation.190 | convolution fusion | flops 75632632 | bytes 9541696 | tf_op jit(solution)/shard_map/dot_general | solution.py:42
  247.1 0.9 fusion.38
  248.0 0.9 multiply_reduce_fusion.24
  249.5 5.8 %multiply_reduce_fusion.23 = (f32[8]{0:T(128)}, f32[8,1536]{1,0:T(8,128)S(1)}) fusion(f32[8,1536]{1,0:T(8,128)S(1)} %get-tuple-element.28, bf16[1536,1536]{1,0:T(8,128)(2,1)} %param.29, bf16[1536,1536]{1,0:T(8,128)(2,1)} %param.28, f32[8]{0:T(128)} %add_rsqrt_fusion.23, f32[1536]{0:T(1024)S(1)} %copy-done.3), kind=kOutput, calls=%fused_computation.185 | convolution fusion | flops 75632632 | bytes 9541696 | tf_op jit(solution)/shard_map/dot_general | solution.py:42
  255.9 0.9 fusion.37
  257.3 5.8 %multiply_reduce_fusion.21 = (f32[8]{0:T(128)}, f32[8,1536]{1,0:T(8,128)S(1)}) fusion(f32[8,1536]{1,0:T(8,128)S(1)} %get-tuple-element.32, bf16[1536,1536]{1,0:T(8,128)(2,1)} %param.29, bf16[1536,1536]{1,0:T(8,128)(2,1)} %param.28, f32[8]{0:T(128)S(1)} %add_rsqrt_fusion.21, f32[1536]{0:T(1024)S(1)} %copy-done.3), kind=kOutput, calls=%fused_computation.180 | convolution fusion | flops 75632632 | bytes 9541696 | tf_op jit(solution)/shard_map/dot_general | solution.py:42
  264.2 5.3 multiply_reduce_fusion.19
  270.0 5.3 multiply_reduce_fusion.17
  275.5 17.3 %all_gather.13 = f32[128,16]{1,0:T(8,128)S(1)} all-gather(f32[8,16]{1,0:T(8,128)S(1)} %fusion.34), channel_id=1, replica_groups=mesh['group'=2,'tensor'=16] {'tensor'}, dimensions={0}, use_global_device_ids=true | all-gather | bytes 8704 | tf_op jit(solution)/shard_map/all_gather | solution.py:141
  292.8 0.7 gather_fusion
  294.3 31.4 %psum.30 = f32[32]{0:T(128)S(1)} all-reduce(f32[32]{0:T(128)S(1)} %get-tuple-element.43), channel_id=1, replica_groups=mesh['group'=2,'tensor'=16] {'tensor'}, use_global_device_ids=true, to_apply=%region_25.26 | all-reduce | flops 32 | bytes 256 | tf_op jit(solution)/shard_map/psum | solution.py:111
  325.7 4.2 fusion.73
  329.9 68.6 %all-reduce.8 = bf16[32,7168]{1,0:T(8,128)(2,1)} all-reduce(f32[32,7168]{1,0:T(8,128)} %fusion.73), channel_id=3, replica_groups=mesh['group'=2,'tensor'=16] {'tensor'}, use_global_device_ids=true, to_apply=%region_26.27.clone | all-reduce | flops 229376 | bytes 1376256
  398.5 0.9 dynamic-slice_convert_fusion
  399.7 1.4 fusion.261
  401.4 1.3 fusion.42
  402.9 19.6 %all-gather.1 = bf16[16,2,5120]{2,1,0:T(2,128)(2,1)} all-gather(bf16[1,2,5120]{2,1,0:T(2,128)(2,1)S(1)} %reshape.393), channel_id=1, replica_groups=mesh['group'=2,'tensor'=16] {'tensor'}, dimensions={0}, use_global_device_ids=true | all-gather | bytes 348160 | tf_op jit(solution)/shard_map/all_gather | solution.py:127
  422.5 1.8 reshape.394
  424.4 2.0 fusion.23
  426.4 2.2 fusion.264
  428.6 61.5 %all-reduce.9 = bf16[32,1536]{1,0:T(8,128)(2,1)S(1)} all-reduce(f32[32,1536]{1,0:T(8,128)} %fusion.264), channel_id=1, replica_groups=mesh['group'=2,'tensor'=16] {'tensor'}, use_global_device_ids=true, to_apply=%region_31.32 | all-reduce | flops 49152 | bytes 294912 | tf_op jit(solution)/shard_map/psum | solution.py:132
  490.1 0.8 fusion.16
  490.9 1.0 multiply_reduce_fusion.15
  492.4 5.8 %multiply_reduce_fusion.14 = (f32[8]{0:T(128)}, f32[8,1536]{1,0:T(8,128)S(1)}) fusion(f32[8,1536]{1,0:T(8,128)S(1)} %get-tuple-element.50, bf16[1536,1536]{1,0:T(8,128)(2,1)} %param.29, bf16[1536,1536]{1,0:T(8,128)(2,1)} %param.28, f32[8]{0:T(128)} %add_rsqrt_fusion.15, f32[1536]{0:T(1024)S(1)} %copy-done.3), kind=kOutput, calls=%fused_computation.163 | convolution fusion | flops 75632632 | bytes 9541696 | tf_op jit(solution)/shard_map/dot_general | solution.py:42
  498.3 0.7 add_rsqrt_fusion.14
  499.0 0.9 fusion.33
  499.8 0.9 multiply_reduce_fusion.13
  500.8 5.3 multiply_reduce_fusion.12
  506.5 5.3 multiply_reduce_fusion.10
  512.3 5.3 multiply_reduce_fusion.8
  518.0 5.3 multiply_reduce_fusion.6
  523.8 5.3 multiply_reduce_fusion.4
  529.5 5.3 multiply_reduce_fusion.2
  535.3 5.3 multiply_reduce_fusion
  540.7 17.3 %all_gather.15 = f32[128,16]{1,0:T(8,128)S(1)} all-gather(f32[8,16]{1,0:T(8,128)S(1)} %fusion.26), channel_id=1, replica_groups=mesh['group'=2,'tensor'=16] {'tensor'}, dimensions={0}, use_global_device_ids=true | all-gather | bytes 8704 | tf_op jit(solution)/shard_map/all_gather | solution.py:141
  558.0 0.7 gather_fusion.1
  (155 shorter events, 20.1 us)
Async XLA Ops:
  0.6 146.3 %copy-start = (bf16[5120,320]{0,1:T(8,128)(2,1)S(1)}, bf16[5120,320]{0,1:T(8,128)(2,1)}, u32[]{:S(2)}) copy-start(bf16[5120,320]{0,1:T(8,128)(2,1)} %param.19) | copy-start | bytes 9830404
  4.0 120.1 %copy-start.26 = (pred[2,96]{1,0:T(4,128)(4,1)}, pred[2,96]{1,0:T(4,128)(4,1)S(1)}, u32[]{:S(2)}) copy-start(pred[2,96]{1,0:T(4,128)(4,1)S(1)} %iota_compare_fusion.1) | copy-start | bytes 580
  39.9 229.8 %copy-start.6 = (f32[1536]{0:T(1024)}, f32[1536]{0:T(1024)S(1)}, u32[]{:S(2)}) copy-start(f32[1536]{0:T(1024)S(1)} %pad_maximum_fusion.7) | copy-start | bytes 18436
  40.0 224.0 %copy-start.8 = (f32[1536]{0:T(1024)}, f32[1536]{0:T(1024)S(1)}, u32[]{:S(2)}) copy-start(f32[1536]{0:T(1024)S(1)} %pad_maximum_fusion.6) | copy-start | bytes 18436
  40.1 216.7 %copy-start.10 = (f32[1536]{0:T(1024)}, f32[1536]{0:T(1024)S(1)}, u32[]{:S(2)}) copy-start(f32[1536]{0:T(1024)S(1)} %pad_maximum_fusion.5) | copy-start | bytes 18436
  47.4 99.5 %copy-start.4 = (bf16[32,320]{1,0:T(8,128)(2,1)S(1)}, bf16[32,320]{1,0:T(8,128)(2,1)}, u32[]{:S(2)}) copy-start(bf16[32,320]{1,0:T(8,128)(2,1)} %param.16) | copy-start | bytes 61444
  51.6 161.3 %copy-start.1 = (bf16[16,1536]{1,0:T(8,128)(2,1)S(1)}, bf16[16,1536]{1,0:T(8,128)(2,1)}, u32[]{:S(2)}) copy-start(bf16[16,1536]{1,0:T(8,128)(2,1)} %param.27) | copy-start | bytes 147460
  51.6 162.8 %copy-start.3 = (f32[1536]{0:T(1024)S(1)}, f32[1536]{0:T(1024)}, u32[]{:S(2)}) copy-start(f32[1536]{0:T(1024)} %param.31) | copy-start | bytes 18436
  214.4 6.6 %copy-start.2 = (bf16[1536,16]{0,1:T(8,128)(2,1)S(1)}, bf16[1536,16]{0,1:T(8,128)(2,1)}, u32[]{:S(2)}) copy-start(bf16[1536,16]{0,1:T(8,128)(2,1)} %param.30) | copy-start | bytes 147460
  221.8 1.0 copy-start.20
  230.6 1.0 copy-start.15
  239.3 1.0 copy-start.16
  248.0 1.0 copy-start.17
  256.7 0.6 copy-start.18
  257.3 6.4 %copy-start.19 = (f32[8,16]{1,0:T(8,128)S(1)}, f32[8,16]{1,0:T(8,128)}, u32[]{:S(2)}) copy-start(f32[8,16]{1,0:T(8,128)} %copy-done.18) | copy-start | bytes 1540
  270.0 24.1 %copy-start.21 = (bf16[16,320]{1,0:T(8,128)(2,1)S(1)}, bf16[16,320]{1,0:T(8,128)(2,1)}, u32[]{:S(2)}) copy-start(bf16[16,320]{1,0:T(8,128)(2,1)} %param.24) | copy-start | bytes 30724
  270.0 55.7 %copy-start.22 = (f32[320]{0:T(512)S(1)}, f32[320]{0:T(512)}, u32[]{:S(2)}) copy-start(f32[320]{0:T(512)} %param.17) | copy-start | bytes 3844
  275.3 124.3 %copy-start.24 = (bf16[2,1,8,128]{3,1,2,0:T(2,128)(2,1)S(1)}, bf16[2,1,8,128]{3,1,2,0:T(2,128)(2,1)}, u32[]{:S(2)}) copy-start(bf16[2,1,8,128]{3,1,2,0:T(2,128)(2,1)} %concatenate.62) | copy-start | bytes 12292
  275.3 124.4 %copy-start.27 = (pred[2,96]{1,0:T(4,128)(4,1)S(1)}, pred[2,96]{1,0:T(4,128)(4,1)}, u32[]{:S(2)}) copy-start(pred[2,96]{1,0:T(4,128)(4,1)} %copy-done.26) | copy-start | bytes 580
  275.3 127.3 %copy-start.23 = (bf16[2,1,8,128]{3,1,2,0:T(2,128)(2,1)S(1)}, bf16[2,1,8,128]{3,1,2,0:T(2,128)(2,1)}, u32[]{:S(2)}) copy-start(bf16[2,1,8,128]{3,1,2,0:T(2,128)(2,1)} %concatenate.64) | copy-start | bytes 12292
  426.4 71.9 %copy-start.5 = (bf16[32,320]{1,0:T(8,128)(2,1)}, bf16[32,320]{1,0:T(8,128)(2,1)S(1)}, u32[]{:S(2)}) copy-start(bf16[32,320]{1,0:T(8,128)(2,1)S(1)} %fusion.23) | copy-start | bytes 61444
  500.8 5.5 copy-start.14
  506.5 5.5 copy-start.13
  512.3 5.5 copy-start.12
  518.0 5.5 copy-start.11
  523.8 5.5 copy-start.9
  529.5 5.5 copy-start.7
  535.3 23.5 %copy-start.25 = (f32[1,2,16]{2,1,0:T(2,128)S(1)}, f32[1,2,16]{2,1,0:T(2,128)}, u32[]{:S(2)}) copy-start(f32[1,2,16]{2,1,0:T(2,128)} %dynamic-slice_bitcast_fusion.1) | copy-start | bytes 388
where the time goes:
time: 561 us; the launch traced here: 559 us
  blocking collectives  401 us (71%)
  matrix products  128 us (23%)
  other arithmetic  18.4 us (3%)
  local copies, waits for them, and re-layouts  10.8 us (2%)
    unnamed x2, blocking collectives  137 us
    psum x2, blocking collectives, per_device(): lax.psum(jnp.dot(decoded, w_cond, preferred_element_type=jnp.float32), 't...  123 us
    dot_general x16, matrix products, denoise(): block = act + jnp.dot(inner, w_down, preferred_element_type=jnp.float32)  87.9 us
    psum x2, blocking collectives, per_device(): squares = lax.psum(jnp.sum(floats * floats, axis=1), 'tensor')  66.3 us
    all_gather x2, blocking collectives, per_device(): lax.all_gather(attended, 'tensor', axis=0, tiled=True)  39.1 us
    all_gather x2, blocking collectives, per_device(): slots_all = lax.all_gather(latent, 'tensor', axis=0, tiled=True)  34.6 us

commit v1 on v0

v1 whole, which is shorter than its diff:
```python
import functools
import math

import numpy as np

import jax
import jax.numpy as jnp
from jax import lax
from jax.experimental import pallas as pl
from jax.experimental.pallas import tpu as pltpu
from jax.sharding import PartitionSpec as P

D = 5120
HEADS = 40
KVH = 8
HD = 128
GRP = HEADS // KVH
HW = 1536
LAT = 16
STEPS = 8
HCAP = 8
LANE = 128
F32 = jnp.float32
BF16 = jnp.bfloat16

QROWS = 128
AROWS = (80, 96)
CROWS = 32
NPHASE = 8
NOISE, QKV, WSUM, WALL = 0, 1, 2, 3


def time_tables():
    half = HW // 2
    freqs = np.exp(-math.log(10000.0) * np.arange(half, dtype=np.float64) / half)
    angle = 1000.0 * np.arange(STEPS, dtype=np.float64)[:, None] / STEPS * freqs[None, :]
    return np.concatenate([np.sin(angle), np.cos(angle)], axis=1).astype(np.float32)


def column_tile(t, j):
    if t < GRP:
        return GRP * j + t
    return HEADS + (t - GRP) * KVH + j


def dot(a, b):
    return jnp.dot(a, b, preferred_element_type=F32)


def dot_t(a, b):
    return lax.dot_general(a, b, (((1,), (1,)), ((), ())), preferred_element_type=F32)


def kernel(
    n,
    tiles,
    x_ref,
    gain_ref,
    wqkv_hbm,
    wout_hbm,
    ck_hbm,
    cv_hbm,
    kvl_ref,
    wcond_hbm,
    wemb_ref,
    plc_ref,
    noise_ref,
    wlat_ref,
    wup_hbm,
    wdown_hbm,
    wvel_ref,
    hgain_ref,
    table_ref,
    lat_out,
    hid_out,
    wqkv,
    wout,
    ck,
    cv,
    wcond,
    wup,
    wdown,
    qkv32,
    qkv_send,
    qkv_recv,
    w_send,
    w_recv,
    w_all,
    noise_all,
    att0_all,
    att1_all,
    att32,
    gathered,
    cond32,
    cond_send0,
    cond_send1,
    cond_recv0,
    cond_recv1,
    cond_own,
    load_sem,
    send_sem,
    recv_sem,
):
    me = lax.axis_index("tensor")
    rows = x_ref.shape[0]

    loads = [
        pltpu.make_async_copy(src, dst, load_sem.at[k])
        for k, (src, dst) in enumerate(
            [
                (wqkv_hbm, wqkv),
                (ck_hbm, ck),
                (cv_hbm, cv),
                (wout_hbm, wout),
                (wcond_hbm, wcond),
                (wup_hbm, wup),
                (wdown_hbm, wdown),
            ]
        )
    ]
    for load in loads:
        load.start()

    barrier = pltpu.get_barrier_semaphore()

    def greet(k, c):
        peer = lax.rem(me + k, n)
        pl.semaphore_signal(
            barrier, inc=1, device_id={"tensor": peer}, device_id_type=pl.DeviceIdType.MESH
        )
        return c

    lax.fori_loop(1, n, greet, 0)

    def block(ref, index, size):
        return ref.at[pl.ds(pl.multiple_of(index * size, size), size), :]

    def copy(phase, src, dst, peer, origin):
        return pltpu.make_async_remote_copy(
            src_ref=src,
            dst_ref=dst,
            send_sem=send_sem.at[phase, peer],
            recv_sem=recv_sem.at[phase, origin],
            device_id={"tensor": peer},
            device_id_type=pl.DeviceIdType.MESH,
        )

    def gather_start(phase, buf, size):
        def body(k, c):
            peer = lax.rem(me + k, n)
            copy(phase, block(buf, me, size), block(buf, me, size), peer, me).start()
            return c

        lax.fori_loop(1, n, body, 0)

    def gather_wait(phase, buf, size):
        def body(k, c):
            peer = lax.rem(me + n - k, n)
            copy(phase, block(buf, me, size), block(buf, peer, size), peer, peer).wait()
            return c

        lax.fori_loop(1, n, body, 0)

    def scatter_start(phase, wide, send, recv, size):
        def body(k, c):
            peer = lax.rem(me + k, n)
            if wide is not None:
                block(send, peer, size)[...] = block(wide, peer, size)[...].astype(BF16)
            copy(phase, block(send, peer, size), block(recv, me, size), peer, me).start()
            return c

        lax.fori_loop(1, n, body, 0)

    def scatter_sum(phase, own, send, recv, size):
        def body(k, acc):
            peer = lax.rem(me + n - k, n)
            copy(phase, block(send, peer, size), block(recv, peer, size), peer, peer).wait()
            return acc + block(recv, peer, size)[...].astype(F32)

        return lax.fori_loop(1, n, body, own)

    to = lax.broadcasted_iota(jnp.int32, (rows, rows), 0)
    frm = lax.broadcasted_iota(jnp.int32, (rows, rows), 1)
    perm = jnp.where(frm == lax.rem(to, n) * 2 + to // n, 1.0, 0.0).astype(BF16)
    back = jnp.where(to == lax.rem(frm, n) * 2 + frm // n, 1.0, 0.0).astype(BF16)

    x0 = dot(perm, x_ref[...])
    squares = jnp.sum(x0 * x0, axis=1, keepdims=True)
    squares = jnp.broadcast_to(squares, (rows, LANE))
    high = squares.astype(BF16).astype(F32)
    embed = wemb_ref[...]
    gain = gain_ref[...]
    left = jnp.concatenate(
        [(x0 * gain).astype(BF16), (embed.astype(F32) * gain).astype(BF16)], axis=0
    )

    block(noise_all, me, HCAP)[...] = jnp.concatenate(
        [noise_ref[0], noise_ref[1], jnp.zeros((HCAP, LANE - 2 * LAT), F32)], axis=1
    )

    pl.semaphore_wait(barrier, n - 1)
    gather_start(NOISE, noise_all, HCAP)

    def place(value, row):
        for i in range(2):
            qkv32[pl.ds(row + i * 8, n, stride=QROWS), :] = value[i * n : (i + 1) * n, :]

    for j in range(KVH):
        place(high if j == 0 else squares - high, 7 * 16 + j)

    loads[0].wait()
    where_to = {column_tile(t, j): (t, j) for t in range(7) for j in range(KVH)}
    wide = 512
    for c in range(0, wqkv.shape[1], wide):
        part = dot(left, wqkv[:, c : c + wide])
        for s in range(wide // LANE):
            t, j = where_to[c // LANE + s]
            piece = part[:, s * LANE : (s + 1) * LANE]
            place(piece[:rows], t * 16 + j)
            at = (t * KVH + j) * LAT
            w_send[at : at + LAT, :] = piece[rows:].astype(BF16)
    scatter_start(QKV, qkv32, qkv_send, qkv_recv, QROWS)

    gram = dot_t(embed, embed)
    gram = jnp.concatenate([gram, jnp.zeros((LAT, LANE - LAT), F32)], axis=1)
    gram_high = gram.astype(BF16)
    w_send[56 * LAT : 57 * LAT, :] = gram_high
    w_send[57 * LAT : 58 * LAT, :] = (gram - gram_high.astype(F32)).astype(BF16)
    w_send[58 * LAT :, :] = jnp.zeros((w_send.shape[0] - 58 * LAT, LANE), BF16)
    cond32[...] = jnp.zeros(cond32.shape, F32)

    gather_wait(NOISE, noise_all, HCAP)
    owner = plc_ref[...].astype(F32)
    index = lax.broadcasted_iota(jnp.int32, (rows, 1), 0)
    slots = lax.broadcasted_iota(jnp.int32, (n * HCAP, 1), 0).astype(F32)
    picked = []
    for i in range(2):
        row = me * 2 + i
        mine = jnp.sum(jnp.where(index == row, owner, 0.0), axis=0, keepdims=True)
        before = jnp.where((owner == mine) & (index < row), 1.0, 0.0)
        slot = mine * HCAP + jnp.sum(before, axis=0, keepdims=True)
        picked.append(
            jnp.sum(jnp.where(slots == slot, noise_all[...], 0.0), axis=0, keepdims=True)
        )
    picked = jnp.concatenate(picked + [jnp.zeros((6, LANE), F32)], axis=0)

    sums = scatter_sum(QKV, block(qkv32, me, QROWS)[...], qkv_send, qkv_recv, QROWS)
    loads[1].wait()
    loads[2].wait()

    head = lax.broadcasted_iota(jnp.int32, (HEADS, LANE), 0) % KVH
    scale = 1.0 / math.sqrt(HD)

    def per_head(value):
        return jnp.concatenate([value] * GRP, axis=0)

    def attend(i, query, extra):
        spread = jnp.concatenate(
            [jnp.where(head == k, query, 0.0) for k in range(KVH)], axis=1
        ).astype(BF16)
        score = dot_t(spread, ck[i]) * scale
        slot = lax.broadcasted_iota(jnp.int32, score.shape, 1)
        score = jnp.where(slot < kvl_ref[i], score, -1e30)
        own = [jnp.sum(query * per_head(k), axis=1, keepdims=True) * scale for k, _ in extra]
        top = jnp.max(score, axis=1, keepdims=True)
        for s in own:
            top = jnp.maximum(top, s)
        prob = jnp.exp(score - top)
        prob_own = [jnp.exp(s - top) for s in own]
        total = jnp.sum(prob, axis=1, keepdims=True)
        for p in prob_own:
            total = total + p
        full = dot((prob / total).astype(BF16), cv[i])
        mixed = jnp.zeros((HEADS, LANE), F32)
        for k in range(KVH):
            mixed = mixed + jnp.where(head == k, full[:, k * LANE : (k + 1) * LANE], 0.0)
        for p, (_, v) in zip(prob_own, extra):
            mixed = mixed + (p / total).astype(BF16).astype(F32) * per_head(v)
        return mixed

    def rounded(value):
        return value.astype(BF16).astype(F32)

    def split(tile_of, inverse, i):
        part = [rounded(tile_of(t, i) * inverse) for t in range(7)]
        return jnp.concatenate(part[:GRP], axis=0), part[GRP], part[GRP + 1]

    def mixed_rows(outs):
        return jnp.concatenate(
            [outs[i][t * 8 : (t + 1) * 8] for t in range(GRP) for i in range(2)], axis=0
        ).astype(BF16)

    def project(att_all, size, inputs):
        att32[pl.ds(0, n * size), :] = att_all[...].astype(F32)
        for t in range(GRP):
            for j in range(KVH):
                h = GRP * j + t
                both = [
                    att32[pl.ds(t * 16 + i * 8 + j, n, stride=size), :] for i in range(2)
                ]
                gathered[:, h * LANE : (h + 1) * LANE] = jnp.concatenate(both, axis=0).astype(
                    BF16
                )
        if inputs is None:
            both = [att32[pl.ds(80 + i * 8, n, stride=size), :] for i in range(2)]
            tokens = jnp.concatenate(both, axis=0)[:, :LAT].astype(BF16)
            inputs = rounded(dot(tokens, embed))
        return (inputs + dot(gathered[...], wout[...])).astype(BF16)

    def send_condition(phase, decoded, send, recv):
        cond = dot(decoded, wcond[...])
        for u in range(HW // LANE):
            for i in range(2):
                cond32[pl.ds(u * 2 + i, n, stride=CROWS), :] = cond[
                    i * n : (i + 1) * n, u * LANE : (u + 1) * LANE
                ]
        scatter_start(phase, cond32, send, recv, CROWS)

    def take_condition(phase, send, recv):
        total = scatter_sum(phase, block(cond32, me, CROWS)[...], send, recv, CROWS)
        total = rounded(total)
        cond_own[...] = jnp.zeros(cond_own.shape, F32)
        for u in range(HW // LANE):
            cond_own[0:2, u * LANE : (u + 1) * LANE] = total[2 * u : 2 * u + 2, :]

    def denoise(first, last, latent):
        def body(k, latent):
            act = dot(latent.astype(BF16), wlat_ref[...])
            act = act + cond_own[...] + table_ref[pl.ds(k, 1), :]
            inv = lax.rsqrt(jnp.mean(act * act, axis=1, keepdims=True) + 1e-05)
            norm = (act * inv * hgain_ref[...]).astype(BF16)
            inner = jax.nn.silu(dot(norm, wup[...])).astype(BF16)
            out = act + dot(inner, wdown[...])
            inv = lax.rsqrt(jnp.mean(out * out, axis=1, keepdims=True) + 1e-05)
            return latent + dot((out * inv).astype(BF16), wvel_ref[...]) / STEPS

        return lax.fori_loop(first, last, body, latent)

    outs, kept = [], []
    for i in range(2):
        base = 7 * 16 + i * 8
        square = sums[base : base + 1, 0:1] + sums[base + 1 : base + 2, 0:1]
        inverse = 1.0 / jnp.sqrt(square / D + 1e-06)
        query, key, value = split(
            lambda t, i: sums[t * 16 + i * 8 : t * 16 + i * 8 + 8], inverse, i
        )
        kept.append((key, value))
        outs.append(attend(i, query, [(key, value)]))
    block(att0_all, me, AROWS[0])[...] = mixed_rows(outs)
    gather_start(4, att0_all, AROWS[0])
    loads[3].wait()
    loads[4].wait()
    gather_wait(4, att0_all, AROWS[0])
    decoded = project(att0_all, AROWS[0], x0)
    send_condition(5, decoded, cond_send0, cond_recv0)
    scatter_start(WSUM, None, w_send, w_recv, tiles * LAT)
    loads[5].wait()
    loads[6].wait()
    take_condition(5, cond_send0, cond_recv0)
    latent = denoise(0, STEPS // 2, picked[:, :LAT])
    size = tiles * LAT
    total = scatter_sum(WSUM, block(w_send, me, size)[...].astype(F32), w_send, w_recv, size)
    block(w_all, me, size)[...] = total.astype(BF16)
    gather_start(WALL, w_all, size)
    latent = denoise(STEPS // 2, STEPS, latent)
    lat_out[0] = latent[0:2]
    gather_wait(WALL, w_all, size)

    token = latent.astype(BF16)
    form = dot(token, w_all[56 * LAT : 57 * LAT, :]) + dot(token, w_all[57 * LAT : 58 * LAT, :])
    square = jnp.sum(form[:, :LAT] * token.astype(F32), axis=1, keepdims=True)
    inverse = 1.0 / jnp.sqrt(jnp.maximum(square, 0.0) / D + 1e-06)
    token = token.astype(F32)
    lane = lax.broadcasted_iota(jnp.int32, (KVH, LANE), 1) // LAT
    which = lax.broadcasted_iota(jnp.int32, (KVH, LANE), 0)
    spread = []
    for i in range(2):
        eight = jnp.concatenate([token[i : i + 1, :]] * KVH, axis=1)
        spread.append(jnp.where(lane == which, jnp.broadcast_to(eight, (KVH, LANE)), 0.0))
    spread = jnp.concatenate(spread, axis=0).astype(BF16)
    second = [dot(spread, w_all[t * LANE : (t + 1) * LANE, :]) for t in range(7)]
    outs = []
    for i in range(2):
        query, key, value = split(
            lambda t, i: second[t][i * 8 : i * 8 + 8], inverse[i : i + 1], i
        )
        outs.append(attend(i, query, [kept[i], (key, value)]))
    sent = jnp.concatenate(
        [token, jnp.zeros((8, LANE - LAT), F32)], axis=1
    )
    sent = [jnp.broadcast_to(sent[i : i + 1, :], (8, LANE)) for i in range(2)]
    block(att1_all, me, AROWS[1])[...] = jnp.concatenate(
        [mixed_rows(outs), jnp.concatenate(sent, axis=0).astype(BF16)], axis=0
    )
    gather_start(6, att1_all, AROWS[1])
    gather_wait(6, att1_all, AROWS[1])
    decoded = project(att1_all, AROWS[1], None)
    send_condition(7, decoded, cond_send1, cond_recv1)
    hid_out[...] = dot(back, decoded).astype(BF16)
    take_condition(7, cond_send1, cond_recv1)
    latent = denoise(0, STEPS, picked[:, LAT : 2 * LAT])
    lat_out[1] = latent[0:2]


def per_device(
    tokens_in,
    norm_gain,
    w_qkv,
    w_out,
    cache_keys,
    cache_values,
    kv_lengths,
    w_cond,
    w_embed,
    placement,
    noise,
    w_latent,
    w_up,
    w_down,
    w_vel,
    head_gain,
):
    n = lax.axis_size("tensor")
    rows, own = tokens_in.shape
    tiles = -(-64 // n)
    total = tiles * n
    vmem = pl.BlockSpec(memory_space=pltpu.VMEM)
    smem = pl.BlockSpec(memory_space=pltpu.SMEM)
    hbm = pl.BlockSpec(memory_space=pl.ANY)
    scratch = [
        pltpu.VMEM(w_qkv.shape, BF16),
        pltpu.VMEM(w_out.shape, BF16),
        pltpu.VMEM(cache_keys.shape, BF16),
        pltpu.VMEM(cache_values.shape, BF16),
        pltpu.VMEM(w_cond.shape, BF16),
        pltpu.VMEM(w_up.shape, BF16),
        pltpu.VMEM(w_down.shape, BF16),
        pltpu.VMEM((n * QROWS, LANE), F32),
        pltpu.VMEM((n * QROWS, LANE), BF16),
        pltpu.VMEM((n * QROWS, LANE), BF16),
        pltpu.VMEM((total * LAT, LANE), BF16),
        pltpu.VMEM((total * LAT, LANE), BF16),
        pltpu.VMEM((total * LAT, LANE), BF16),
        pltpu.VMEM((n * HCAP, LANE), F32),
        pltpu.VMEM((n * AROWS[0], LANE), BF16),
        pltpu.VMEM((n * AROWS[1], LANE), BF16),
        pltpu.VMEM((n * AROWS[1], LANE), F32),
        pltpu.VMEM((rows, D), BF16),
        pltpu.VMEM((n * CROWS, LANE), F32),
        pltpu.VMEM((n * CROWS, LANE), BF16),
        pltpu.VMEM((n * CROWS, LANE), BF16),
        pltpu.VMEM((n * CROWS, LANE), BF16),
        pltpu.VMEM((n * CROWS, LANE), BF16),
        pltpu.VMEM((8, HW), F32),
        pltpu.SemaphoreType.DMA((7,)),
        pltpu.SemaphoreType.DMA((NPHASE, n)),
        pltpu.SemaphoreType.DMA((NPHASE, n)),
    ]
    return pl.pallas_call(
        functools.partial(kernel, n, tiles),
        out_shape=(
            jax.ShapeDtypeStruct((2, rows // n, LAT), F32),
            jax.ShapeDtypeStruct((rows, own), BF16),
        ),
        in_specs=[
            vmem, vmem, hbm, hbm, hbm, hbm, smem, hbm, vmem, vmem, vmem, vmem, hbm, hbm, vmem,
            vmem, vmem,
        ],
        out_specs=(vmem, vmem),
        scratch_shapes=scratch,
        compiler_params=pltpu.CompilerParams(
            collective_id=0, has_side_effects=True, vmem_limit_bytes=50 * 1024 * 1024
        ),
    )(
        tokens_in,
        norm_gain[None, :],
        w_qkv,
        w_out,
        cache_keys,
        cache_values,
        kv_lengths,
        w_cond,
        w_embed,
        placement,
        noise,
        w_latent,
        w_up,
        w_down,
        w_vel,
        head_gain[None, :],
        jnp.asarray(time_tables()),
    )


def solution(mesh):
    return jax.shard_map(
        per_device,
        mesh=mesh,
        in_specs=(
            P("group", "tensor"),
            P("tensor"),
            P("tensor", None),
            P(None, "tensor"),
            P(("group", "tensor"), None, None),
            P(("group", "tensor"), None, None),
            P(("group", "tensor")),
            P("tensor", None),
            P(None, "tensor"),
            P("group", None),
            P(None, ("group", "tensor"), None),
            P(),
            P(),
            P(),
            P(),
            P(),
        ),
        out_specs=(P(None, ("group", "tensor"), None), P("group", "tensor")),
        check_vma=False,
    )
```

time: 561 us -> 99.4 us (0.18)
  blocking collectives: 401 us -> 0 us
  matrix products: 128 us -> 0 us
  Pallas kernels: 0 us -> 87.9 us
  other arithmetic: 18.4 us -> 0 us
    psum x4 -> x0, blocking collectives: 190 us -> none  [the longest x2 123 us: per_device(): lax.psum(jnp.dot(decoded, w_cond, preferred_element_type=jnp.float32), 't...]
    unnamed x2 -> x0, blocking collectives: 137 us -> none
    dot_general x63 -> x0, matrix products: 128 us -> none  [the longest x16 87.9 us: denoise(): block = act + jnp.dot(inner, w_down, preferred_element_type=jnp.float32)]
    pallas_call x0 -> x1, Pallas kernels: none -> 87.9 us  [per_device(): pl.pallas_call(functools.partial(kernel, n, tiles), out_shape=(jax.ShapeD...]
    all_gather x4 -> x0, blocking collectives: 73.7 us -> none  [the longest x2 39.1 us: per_device(): lax.all_gather(attended, 'tensor', axis=0, tiled=True)]
    rsqrt x32 -> x0, other arithmetic: 7.77 us -> none  [the longest x16 4.49 us: denoise(): lax.rsqrt(jnp.mean(block * block, axis=1, keepdims=True) + 1e-05)]
where the time goes in v1:
time: 99.4 us; the launch traced here: 99 us
  Pallas kernels  87.9 us (88%)
  local copies, waits for them, and re-layouts  10.4 us (10%)
    pallas_call x1, Pallas kernels, per_device(): pl.pallas_call(functools.partial(kernel, n, tiles), out_shape=(jax.ShapeD...  87.9 us
    unnamed x23, local copies, waits for them, and re-layouts  8.85 us

profile of v1, /device:TPU:0, one launch (start us, length us, event | category | flops | bytes accessed | tf_op | source)
XLA Modules:
  0.0 99.0 jit_solution(8728580957926041689)
XLA Ops:
  0.6 0.0 copy-start.4
  0.6 0.0 copy-start.3
  0.7 0.0 copy-start.7
  0.7 0.0 copy-start.6
  0.7 0.0 copy-start
  0.7 0.0 copy-start.8
  0.7 0.0 copy-start.2
  0.7 0.0 copy-start.1
  0.7 0.0 copy-start.5
  0.7 0.8 broadcast_in_dim.6.gain_ref
  1.5 0.7 broadcast_in_dim.7.hgain_ref
  2.2 0.7 copy.20.plc_ref
  3.0 1.0 %copy.21.wvel_ref = bf16[1536,16]{1,0:T(8,128)(2,1)S(1)} copy(bf16[1536,16]{0,1:T(8,128)(2,1)} %param.31) | data formatting | bytes 98304 | tf_op args[14]
  4.0 5.9 %copy.19.wout_hbm = bf16[5120,320]{1,0:T(8,128)(2,1)} copy(bf16[5120,320]{0,1:T(8,128)(2,1)} %param.20) | data formatting | bytes 6553600 | tf_op args[3]
  9.9 0.0 copy-done.4
  9.9 0.0 copy-done.3
  9.9 0.0 copy-done.7
  9.9 0.0 copy-done.6
  9.9 0.0 copy-done
  9.9 0.0 copy-done.8
  9.9 0.0 copy-done.2
  9.9 0.0 copy-done.1
  9.9 0.0 copy-done.5
  9.9 87.9 %shard_map.176 = (f32[2,2,16]{2,1,0:T(2,128)S(1)}, bf16[32,320]{1,0:T(8,128)(2,1)S(1)}) custom-call(bf16[32,320]{1,0:T(8,128)(2,1)S(1)} %copy-done.5, f32[1,320]{1,0:T(1,128)S(1)} %broadcast_in_dim.6.gain_ref, bf16[320,7168]{1,0:T(8,128)(2,1)} %wqkv_hbm.1, bf16[5120,320]{1,0:T(8,128)(2,1)} %copy.19.wout_hbm, bf16[2,96,1024]{2,1,0:T(8,128)(2,1)S(1)} %copy-done.1, ...), custom_call_target="tpu_custom_call" | custom-call | tf_op jit(solution)/shard_map/pallas_call | solution.py:459
  97.9 0.6 copy.24
  98.4 0.6 copy.25
Async XLA Ops:
  0.6 9.2 %copy-start.4 = (f32[8,1536]{1,0:T(8,128)S(1)}, f32[8,1536]{1,0:T(8,128)}, u32[]{:S(2)}) copy-start(f32[8,1536]{1,0:T(8,128)} %constant.2.clone.table_ref) | copy-start | bytes 147460
  0.6 9.2 %copy-start.3 = (bf16[16,1536]{1,0:T(8,128)(2,1)S(1)}, bf16[16,1536]{1,0:T(8,128)(2,1)}, u32[]{:S(2)}) copy-start(bf16[16,1536]{1,0:T(8,128)(2,1)} %wlat_ref.1) | copy-start | bytes 147460
  0.7 9.2 %copy-start.7 = (f32[2,8,16]{2,1,0:T(8,128)S(1)}, f32[2,8,16]{2,1,0:T(8,128)}, u32[]{:S(2)}) copy-start(f32[2,8,16]{2,1,0:T(8,128)} %noise_ref.1) | copy-start | bytes 3076
  0.7 9.2 %copy-start.6 = (bf16[16,320]{1,0:T(8,128)(2,1)S(1)}, bf16[16,320]{1,0:T(8,128)(2,1)}, u32[]{:S(2)}) copy-start(bf16[16,320]{1,0:T(8,128)(2,1)} %wemb_ref.1) | copy-start | bytes 30724
  0.7 9.2 %copy-start = (bf16[320,1536]{1,0:T(8,128)(2,1)S(1)}, bf16[320,1536]{1,0:T(8,128)(2,1)}, u32[]{:S(2)}) copy-start(bf16[320,1536]{1,0:T(8,128)(2,1)} %wcond_hbm.1) | copy-start | bytes 2949124
  0.7 9.2 %copy-start.8 = (s32[2]{0:T(128)S(1)}, s32[2]{0:T(128)}, u32[]{:S(2)}) copy-start(s32[2]{0:T(128)} %kvl_ref.1) | copy-start | bytes 28
  0.7 9.2 %copy-start.2 = (bf16[2,96,1024]{2,1,0:T(8,128)(2,1)S(1)}, bf16[2,96,1024]{2,1,0:T(8,128)(2,1)}, u32[]{:S(2)}) copy-start(bf16[2,96,1024]{2,1,0:T(8,128)(2,1)} %cv_hbm.1) | copy-start | bytes 1179652
  0.7 9.2 %copy-start.1 = (bf16[2,96,1024]{2,1,0:T(8,128)(2,1)S(1)}, bf16[2,96,1024]{2,1,0:T(8,128)(2,1)}, u32[]{:S(2)}) copy-start(bf16[2,96,1024]{2,1,0:T(8,128)(2,1)} %ck_hbm.1) | copy-start | bytes 1179652
  0.7 9.2 %copy-start.5 = (bf16[32,320]{1,0:T(8,128)(2,1)S(1)}, bf16[32,320]{1,0:T(8,128)(2,1)}, u32[]{:S(2)}) copy-start(bf16[32,320]{1,0:T(8,128)(2,1)} %x_ref.1) | copy-start | bytes 61444

commit v2 on v1

--- a/solution.py
+++ b/solution.py
@@ -189,7 +189,8 @@
     squares = jnp.broadcast_to(squares, (rows, LANE))
     high = squares.astype(BF16).astype(F32)
     embed = wemb_ref[...]
-    gain = gain_ref[...]
+    gain = gain_ref[...][None, :]
+    head_gain = hgain_ref[...][None, :]
     left = jnp.concatenate(
         [(x0 * gain).astype(BF16), (embed.astype(F32) * gain).astype(BF16)], axis=0
     )
@@ -231,14 +232,14 @@
 
     gather_wait(NOISE, noise_all, HCAP)
     owner = plc_ref[...].astype(F32)
-    index = lax.broadcasted_iota(jnp.int32, (rows, 1), 0)
+    index = lax.broadcasted_iota(jnp.int32, (1, rows), 1)
     slots = lax.broadcasted_iota(jnp.int32, (n * HCAP, 1), 0).astype(F32)
     picked = []
     for i in range(2):
         row = me * 2 + i
-        mine = jnp.sum(jnp.where(index == row, owner, 0.0), axis=0, keepdims=True)
+        mine = jnp.sum(jnp.where(index == row, owner, 0.0), axis=1, keepdims=True)
         before = jnp.where((owner == mine) & (index < row), 1.0, 0.0)
-        slot = mine * HCAP + jnp.sum(before, axis=0, keepdims=True)
+        slot = mine * HCAP + jnp.sum(before, axis=1, keepdims=True)
         picked.append(
             jnp.sum(jnp.where(slots == slot, noise_all[...], 0.0), axis=0, keepdims=True)
         )
@@ -305,7 +306,7 @@
             both = [att32[pl.ds(80 + i * 8, n, stride=size), :] for i in range(2)]
             tokens = jnp.concatenate(both, axis=0)[:, :LAT].astype(BF16)
             inputs = rounded(dot(tokens, embed))
-        return (inputs + dot(gathered[...], wout[...])).astype(BF16)
+        return (inputs + dot_t(gathered[...], wout[...])).astype(BF16)
 
     def send_condition(phase, decoded, send, recv):
         cond = dot(decoded, wcond[...])
@@ -328,11 +329,11 @@
             act = dot(latent.astype(BF16), wlat_ref[...])
             act = act + cond_own[...] + table_ref[pl.ds(k, 1), :]
             inv = lax.rsqrt(jnp.mean(act * act, axis=1, keepdims=True) + 1e-05)
-            norm = (act * inv * hgain_ref[...]).astype(BF16)
+            norm = (act * inv * head_gain).astype(BF16)
             inner = jax.nn.silu(dot(norm, wup[...])).astype(BF16)
             out = act + dot(inner, wdown[...])
             inv = lax.rsqrt(jnp.mean(out * out, axis=1, keepdims=True) + 1e-05)
-            return latent + dot((out * inv).astype(BF16), wvel_ref[...]) / STEPS
+            return latent + dot_t((out * inv).astype(BF16), wvel_ref[...]) / STEPS
 
         return lax.fori_loop(first, last, body, latent)
 
@@ -429,7 +430,7 @@
     hbm = pl.BlockSpec(memory_space=pl.ANY)
     scratch = [
         pltpu.VMEM(w_qkv.shape, BF16),
-        pltpu.VMEM(w_out.shape, BF16),
+        pltpu.VMEM(w_out.shape[::-1], BF16),
         pltpu.VMEM(cache_keys.shape, BF16),
         pltpu.VMEM(cache_values.shape, BF16),
         pltpu.VMEM(w_cond.shape, BF16),
@@ -469,25 +470,25 @@
         out_specs=(vmem, vmem),
         scratch_shapes=scratch,
         compiler_params=pltpu.CompilerParams(
-            collective_id=0, has_side_effects=True, vmem_limit_bytes=50 * 1024 * 1024
+            collective_id=0, has_side_effects=True, vmem_limit_bytes=60 * 1024 * 1024
         ),
     )(
         tokens_in,
-        norm_gain[None, :],
+        norm_gain,
         w_qkv,
-        w_out,
+        w_out.T,
         cache_keys,
         cache_values,
         kv_lengths,
         w_cond,
         w_embed,
-        placement,
+        placement.T,
         noise,
         w_latent,
         w_up,
         w_down,
-        w_vel,
-        head_gain[None, :],
+        w_vel.T,
+        head_gain,
         jnp.asarray(time_tables()),
     )
 

time: 99.4 us -> 92.1 us (0.927)
  local copies, waits for them, and re-layouts: 10.4 us -> 2.59 us
    unnamed x23 -> x2, local copies, waits for them, and re-layouts: 8.85 us -> 2.59 us
    broadcast_in_dim x2 -> x0, local copies, waits for them, and re-layouts: 1.51 us -> none  [the longest x1 0.81 us: per_device(): norm_gain[None, :]]
where the time goes in v2:
time: 92.1 us; the launch traced here: 91.9 us
  Pallas kernels  88.6 us (96%)
  local copies, waits for them, and re-layouts  2.59 us (3%)
    pallas_call x1, Pallas kernels, per_device(): pl.pallas_call(functools.partial(kernel, n, tiles), out_shape=(jax.ShapeD...  88.6 us
    unnamed x2, local copies, waits for them, and re-layouts  2.59 us

profile of v2, /device:TPU:0, one launch (start us, length us, event | category | flops | bytes accessed | tf_op | source)
XLA Modules:
  0.0 91.9 jit_solution(15531256363997981989)
XLA Ops:
  0.6 88.6 %shard_map.176 = (f32[2,2,16]{2,1,0:T(2,128)}, bf16[32,320]{1,0:T(8,128)(2,1)}) custom-call(bf16[32,320]{1,0:T(8,128)(2,1)} %x_ref.1, f32[320]{0:T(512)} %gain_ref.1, bf16[320,7168]{1,0:T(8,128)(2,1)} %wqkv_hbm.1, bf16[320,5120]{1,0:T(8,128)(2,1)} %bitcast.3, bf16[2,96,1024]{2,1,0:T(8,128)(2,1)} %ck_hbm.1, bf16[2,96,1024]{2,1,0:T(8,128)(2,1)} %cv_hbm.1, ...), custom_call_target="tpu_custom_call" | custom-call | tf_op jit(solution)/shard_map/pallas_call | solution.py:460
  89.3 1.2 %copy.21 = f32[2,2,16]{2,1,0:T(2,128)} copy(f32[2,2,16]{2,1,0:T(2,128)} %get-tuple-element.4) | data formatting | bytes 512
  90.5 1.3 %copy.22 = bf16[32,320]{1,0:T(8,128)(2,1)} copy(bf16[32,320]{1,0:T(8,128)(2,1)} %get-tuple-element.5) | data formatting | bytes 40960
